TPU v7x, 256 devices: a whole 4x4x8 slice. The times are simulated.
256 devices in a mesh: rcv: 32 (over x, z), src: 8 (over y, core).
Axes of the slice: x: 4, y: 4, z: 8, core: 2. Of those that a mesh axis runs over, the one named last changes fastest.
Arguments:
- reflectivity: bfloat16 [2, 1, 2048, 2048], P(None, None, 'rcv', 'src'), may hold values from -0.09375 to 0.09375
- downgoing: bfloat16 [2, 1, 2048, 4096], P(None, None, 'rcv', 'src'), may hold values from -6 to 6
- upgoing: bfloat16 [2, 1, 2048, 4096], P(None, None, 'rcv', 'src'), may hold values from -6 to 6
- recorded: int32 [256, 20], P('rcv'), may hold values from 0 to 31, as said below
Outputs:
- residual: float32 [2, 1, 2048, 4096], P(None, None, 'rcv', 'src')
- grad_reflect: float32 [2, 1, 2048, 2048], P(None, None, 'rcv', 'src')
- grad_downgoing: float32 [2, 1, 2048, 4096], P(None, None, 'rcv', 'src')
Inputs may be any that keep to these rules, and one draw needn't show every extreme that they name: `recorded`: each row lists 20 distinct source blocks.
All inputs are finite; a program needn't handle non-finite values.
Results may differ from a plain program's by a relative error of at most 0.0003.
Values may be sent and summed in bfloat16 or wider, within the bound.
No kernel may reach another device: no remote copies, remote signals or barrier semaphores. Data moves between devices by JAX's collectives and lax.ppermute only.
A program may use at most 64 MiB of HBM per device.

v0:
```python
import jax
import jax.numpy as jnp
from jax import lax
from jax.experimental import pallas as pl
from jax.experimental.pallas import tpu as pltpu
from jax.sharding import Mesh, PartitionSpec as P

RBLK = 8
SBLK = 128
X, Z, Y, C = 4, 8, 4, 2
BF, F32, I16 = jnp.bfloat16, jnp.float32, jnp.int16
VMEM = pl.BlockSpec(memory_space=pltpu.VMEM)
ANY = pl.BlockSpec(memory_space=pl.ANY)
SMEM = pl.BlockSpec(memory_space=pltpu.SMEM)
PARAMS = pltpu.CompilerParams(vmem_limit_bytes=16 * 1024 * 1024)


def send(value, axis, size, step):
    return lax.ppermute(value, axis, [(i, (i + step) % size) for i in range(size)])


def turn(value, pairs):
    moves = [(x * Y + y, to[0] * Y + to[1]) for (x, y), to in pairs.items()]
    return lax.ppermute(value, ("x", "y"), moves)


def pair_kernel(place, mine, theirs, out):
    out[place[2]] = mine[...].reshape(128, 256)
    out[1 - place[2]] = theirs[...].reshape(128, 256)


def predict_kernel(place, *refs):
    rows, parts, (p0, p1, p2, p3, wave, refl, acc) = refs[:Y], refs[Y : Y + Z], refs[Y + Z :]
    mx, my, mz = place[0], place[1], place[3]
    for k, r in enumerate(rows):
        for c in range(C):
            refl[c, lax.rem(my - k + Y, Y)] = r[c]
    for zr, part in enumerate(parts):
        z = lax.rem(mz - zr + Z, Z)
        wave[z, :, 0:512] = part[0]
        wave[z, :, 512:1024] = part[1]
    total = jnp.zeros((512, 1024), F32)
    for c in range(C):
        w = wave[4 * c : 4 * c + 4].reshape(256, 1024)
        total += jnp.dot(refl[c].reshape(512, 256), w, preferred_element_type=F32)
    acc[...] = total.reshape(X, 128, 1024)
    for k, out in enumerate((p0, p1, p2, p3)):
        x = lax.rem(mx + k, X)
        a, b = acc[x, 0:64, :], acc[x, 64:128, :]
        real, imag = a[:, :512] - b[:, 512:], a[:, 512:] + b[:, :512]
        value = jnp.concatenate([real, imag], axis=0)
        if k:
            encode(value, out)
        else:
            out[...] = value


def residual_kernel(place, p0, p1, p2, p3, up, rec, res, coded):
    recs = rec[...]
    total = p0[...] + decode(p1) + decode(p2) + decode(p3)
    columns = []
    for k in range(X):
        hit = jnp.max(jnp.where(recs == place[4] + k, 1.0, 0.0), axis=1, keepdims=True)
        hit = jnp.broadcast_to(hit, (8, SBLK))
        columns.append(
            jnp.concatenate(
                [jnp.broadcast_to(hit[r : r + 1], (RBLK, SBLK)) for r in range(8)], axis=0
            )
        )
    mask = jnp.concatenate(columns, axis=1)
    parts = [mask * (total[64 * p : 64 * p + 64] - up[p].astype(F32)) for p in range(2)]
    res[0] = parts[0]
    res[1] = parts[1]
    encode(jnp.concatenate(parts, axis=0), coded)


def encode(value, out):
    rows = value.shape[0]
    most = jnp.max(jnp.abs(value), axis=0, keepdims=True)
    code = jnp.ceil(jnp.log2(jnp.maximum(most, 2.0**-100)) * 128.0 + 0.01)
    scaled = value * (jnp.exp2(code * (-1.0 / 128.0)) * 32767.0)
    scaled = jnp.clip(jnp.round(scaled), -32767.0, 32767.0)
    out[0:rows, :] = scaled.astype(jnp.int32).astype(jnp.int16)
    code = jnp.broadcast_to(code, (16, value.shape[1]))
    out[rows : rows + 16, :] = code.astype(jnp.int32).astype(jnp.int16)


def decode(coded):
    rows = coded.shape[0] - 16
    code = coded[rows : rows + 16, :].astype(jnp.int32).astype(F32)[0:1]
    scale = jnp.exp2(code * (1.0 / 128.0)) * (1.0 / 32767.0)
    return coded[0:rows, :].astype(jnp.int32).astype(F32) * scale


def grads_kernel(place, refl, wave, e0, e1, e2, e3, here, two, back, up, down, far, own, other, high, low, sums):
    mx, mc = place[0], place[2]
    for k, e in enumerate((e0, e1, e2, e3)):
        x = lax.rem(mx - k + X, X)
        value = decode(e)
        upper = value.astype(BF)
        lower = (value - upper.astype(F32)).astype(BF)
        for to, v in ((high, upper), (low, lower)):
            to[x, 0:64, 0:512] = v[0:64]
            to[x, 0:64, 512:1024] = v[64:128]
            to[x, 64:128, 0:512] = v[64:128]
            to[x, 64:128, 512:1024] = -v[0:64]
    h, l = high[...].reshape(512, 1024), low[...].reshape(512, 1024)
    for half in range(C):
        r = refl[half].reshape(512, 256)
        dims = (((0,), (0,)), ((), ()))
        g = lax.dot_general(r, h, dims, preferred_element_type=F32)
        g += lax.dot_general(r, l, dims, preferred_element_type=F32)
        for q in range(4):
            part = g[q * 64 : q * 64 + 64]
            part = jnp.concatenate([part[:, 0:512], part[:, 512:1024]], axis=0)
            sums[4 * half + q] = part
    def toward(step):
        return sums[lax.rem(place[3] + step + Z, Z)]

    here[...] = toward(0)
    two[...] = toward(2)
    back[...] = toward(-2)
    encode(toward(1), up.at[0])
    encode(toward(3), up.at[1])
    encode(toward(-1), down.at[0])
    encode(toward(-3), down.at[1])
    encode(toward(4), far)
    for to, half in ((own, mc), (other, 1 - mc)):
        w = wave[pl.ds(4 * half, 4)].reshape(256, 1024)
        dims = (((1,), (1,)), ((), ()))
        g = lax.dot_general(h, w, dims, preferred_element_type=F32)
        g += lax.dot_general(l, w, dims, preferred_element_type=F32)
        to[...] = g.reshape(X, 128, 256)


def core_sum_kernel(place, own, other, s0, s1, s2, s3):
    for k, out in enumerate((s0, s1, s2, s3)):
        x = lax.rem(place[1] + k, X)
        out[...] = own[x] + other[x]


def refl_sum_kernel(place, s0, s1, s2, s3, here, up, down, out, base):
    out[...] = (s0[...] + s1[...]) + (s2[...] + s3[...])
    base[...] = here[...] + decode(up.at[0]) + decode(down.at[0])


def relay_kernel(place, two, back, up, down, after, out_up, out_down):
    encode(two[...] + decode(up.at[1]), out_up)
    encode(back[...] + decode(down.at[1]), out_down)


def last_kernel(scale, refl_scale, place, base, up2, down2, far, grad, out, refl_out):
    total = base[...] + decode(up2) + decode(down2) + decode(far)
    out[...] = (total * scale).reshape(2, 64, 512)
    refl_out[...] = (grad[...] * refl_scale).reshape(2, 64, 256)


def kernel_call(body, outs, ins, name, out_specs=None, aliases={}, scratch=()):
    return pl.pallas_call(
        body,
        out_shape=[jax.ShapeDtypeStruct(s, d) for s, d in outs],
        in_specs=[SMEM] + ins,
        out_specs=out_specs or [VMEM] * len(outs),
        input_output_aliases=aliases,
        scratch_shapes=scratch,
        compiler_params=PARAMS,
        name=name,
    )


def shards(reflectivity, downgoing, upgoing, recorded):
    mx, my, mc = lax.axis_index("x"), lax.axis_index("y"), lax.axis_index("c")
    place = jnp.stack([mx, my, mc, lax.axis_index("z"), (my * C + mc) * X]).astype(jnp.int32)
    n_rec, n_src = Z * X * 64, Y * C * 512
    grid = [(x, y) for x in range(X) for y in range(Y)]

    wave = {0: downgoing[:, 0]}
    wave |= {k % Z: send(wave[0], "z", Z, k) for k in (2, -2, 1, -1)}
    wave[3] = send(wave[2], "z", Z, 1)
    wave[5] = send(wave[6], "z", Z, -1)
    wave[4] = send(wave[2], "z", Z, 2)
    wave = [wave[k] for k in range(Z)]
    refl = reflectivity[:, 0]
    (refl,) = kernel_call(pair_kernel, [((C, 128, 256), BF)], [VMEM] * 2, "pair")(
        place, refl, send(refl, "c", C, 1)
    )
    refl = turn(refl, {(x, y): (y, x) for x, y in grid})
    refl = [refl] + [send(refl, "y", Y, k) for k in range(1, Y)]

    *pred, wave, refl = kernel_call(
        predict_kernel,
        [((128, 512), F32)] + [((144, 512), I16)] * 3 + [((Z, 64, 1024), BF), ((C, X, 128, 256), BF)],
        [VMEM] * 12,
        "predict",
        scratch=[pltpu.VMEM((X, 128, 1024), F32)],
    )(place, *refl, *wave)
    pred = [pred[0]] + [send(pred[k], "x", X, k) for k in range(1, X)]
    residual, coded = kernel_call(
        residual_kernel, [((2, 64, 512), F32), ((144, 512), I16)], [VMEM] * 6, "residual"
    )(place, *pred, upgoing[:, 0], recorded)
    coded = [coded] + [send(coded, "x", X, k) for k in range(1, X)]
    here, two, back, up, down, far, own, other = kernel_call(
        grads_kernel,
        [((128, 512), F32)] * 3
        + [((2, 144, 512), I16)] * 2
        + [((144, 512), I16)]
        + [((X, 128, 256), F32)] * 2,
        [VMEM] * 6,
        "grads",
        scratch=[pltpu.VMEM((X, 128, 1024), BF)] * 2 + [pltpu.VMEM((Z, 128, 512), F32)],
    )(place, refl, wave, *coded)
    up, down, far = send(up, "z", Z, 1), send(down, "z", Z, -1), send(far, "z", Z, 4)
    other = send(other, "c", C, 1)
    sums = kernel_call(core_sum_kernel, [((128, 256), F32)] * X, [VMEM] * 2, "core_sum")(
        place, own, other
    )
    up2, down2 = kernel_call(relay_kernel, [((144, 512), I16)] * 2, [VMEM] * 4 + [ANY], "relay")(
        place, two, back, up, down, sums[0]
    )
    up2, down2 = send(up2, "z", Z, 2), send(down2, "z", Z, -2)

    sums = [sums[0]] + [send(sums[k], "y", Y, k) for k in range(1, Y)]

    def last(*refs):
        last_kernel(n_rec ** (-0.5), n_src ** (-0.5), *refs)

    grad, base = kernel_call(
        refl_sum_kernel, [((128, 256), F32), ((128, 512), F32)], [VMEM] * 7, "refl_sum"
    )(place, *sums, here, up, down)
    grad = turn(grad, {(x, y): (y, x) for x, y in grid})
    grad_downgoing, grad_reflect = kernel_call(
        last, [((2, 64, 512), F32), ((2, 64, 256), F32)], [VMEM] * 5, "last"
    )(place, base, up2, down2, far, grad)
    return residual[:, None], grad_reflect[:, None], grad_downgoing[:, None]


def solution(mesh):
    fine = Mesh(mesh.devices.reshape(X, Z, Y, C), ("x", "z", "y", "c"))
    spec = P(None, None, ("x", "z"), ("y", "c"))
    return jax.shard_map(
        shards,
        mesh=fine,
        in_specs=(spec, spec, spec, P(("x", "z"), None)),
        out_specs=(spec, spec, spec),
        check_vma=False,
    )
```

profile of v0, /device:TPU:1, one launch (start us, length us, event | category | flops | bytes accessed | tf_op | source)
XLA Modules:
  0.0 95.5 jit_solution(7704269565119902005)
XLA Ops:
  0.6 6.9 %collective-permute-start.9 = (bf16[2,64,512]{2,1,0:T(8,128)(2,1)}, bf16[2,64,512]{2,1,0:T(8,128)(2,1)S(1)}, u32[]{:S(2)}, u32[]{:S(2)}) collective-permute-start(bf16[2,64,512]{2,1,0:T(8,128)(2,1)} %bitcast.17), channel_id=1, source_target_pairs={{0,48},{8,56},{16,0},{24,8},{32,16},{40,24},{48,32},{56,40},{1,49}... | collective-permute-start | bytes 393224 | tf_op jit(solution)/shard_map/ppermute | solution.py:19
  7.6 1.0 %collective-permute-start = (bf16[2,64,256]{2,1,0:T(8,128)(2,1)}, bf16[2,64,256]{2,1,0:T(8,128)(2,1)S(1)}, u32[]{:S(2)}, u32[]{:S(2)}) collective-permute-start(bf16[2,64,256]{2,1,0:T(8,128)(2,1)} %bitcast.23), channel_id=1, source_target_pairs={{0,1},{1,0},{2,3},{3,2},{4,5},{5,4},{6,7},{7,6},{8,9},{9,8},{10,11... | collective-permute-start | bytes 196616 | tf_op jit(solution)/shard_map/ppermute | solution.py:19
  8.5 0.7 collective-permute-start.11
  9.2 1.2 %collective-permute-start.6 = (bf16[2,64,512]{2,1,0:T(8,128)(2,1)}, bf16[2,64,512]{2,1,0:T(8,128)(2,1)S(1)}, u32[]{:S(2)}, u32[]{:S(2)}) collective-permute-start(bf16[2,64,512]{2,1,0:T(8,128)(2,1)} %bitcast.19), channel_id=1, source_target_pairs={{0,16},{8,24},{16,32},{24,40},{32,48},{40,56},{48,0},{56,8},{1,17}... | collective-permute-start | bytes 393224 | tf_op jit(solution)/shard_map/ppermute | solution.py:19
  10.4 0.1 stack.23.place.refs_0_
  10.5 0.0 collective-permute-done.theirs
  10.5 0.9 copy-done.2
  11.4 0.6 pair.1
  12.0 0.0 copy-start.1
  12.0 0.8 collective-permute-start.1
  12.8 0.1 collective-permute-start.5
  12.9 0.0 collective-permute-done.9.refs_10_
  12.9 3.1 %collective-permute-start.10 = (bf16[2,64,512]{2,1,0:T(8,128)(2,1)S(1)}, bf16[2,64,512]{2,1,0:T(8,128)(2,1)S(1)}, u32[]{:S(2)}, u32[]{:S(2)}) collective-permute-start(bf16[2,64,512]{2,1,0:T(8,128)(2,1)S(1)} %collective-permute-done.9.refs_10_), channel_id=1, source_target_pairs={{0,56},{8,0},{16,8},{24,16},{32,24},{40,32},{48,40},{56,48},{1,57}... | collective-permute-start | bytes 393224 | tf_op jit(solution)/shard_map/ppermute | solution.py:19
  16.0 3.5 %collective-permute-done.6.refs_6_ = bf16[2,64,512]{2,1,0:T(8,128)(2,1)S(1)} collective-permute-done((bf16[2,64,512]{2,1,0:T(8,128)(2,1)}, bf16[2,64,512]{2,1,0:T(8,128)(2,1)S(1)}, u32[]{:S(2)}, u32[]{:S(2)}) %collective-permute-start.6) | collective-permute-done | bytes 131104 | tf_op jit(solution)/shard_map/ppermute | solution.py:19
  19.5 0.0 collective-permute-start.8
  19.5 0.0 collective-permute-done.11.refs_11_
  19.5 0.0 collective-permute-start.7
  19.6 0.0 collective-permute-done.1.refs_0_
  19.6 8.2 %collective-permute-start.4 = (bf16[2,128,256]{2,1,0:T(8,128)(2,1)S(1)}, bf16[2,128,256]{2,1,0:T(8,128)(2,1)S(1)}, u32[]{:S(2)}, u32[]{:S(2)}) collective-permute-start(bf16[2,128,256]{2,1,0:T(8,128)(2,1)S(1)} %collective-permute-done.1.refs_0_), channel_id=1, source_target_pairs={{0,6},{2,0},{4,2},{6,4},{1,7},{3,1},{5,3},{7,5},{8,14},{10,8},{12,... | collective-permute-start | bytes 393224 | tf_op jit(solution)/shard_map/ppermute | solution.py:19
  27.8 0.0 collective-permute-done.5.refs_5_
  27.8 0.0 collective-permute-start.3
  27.8 0.0 collective-permute-done.10.refs_9_
  27.8 0.6 collective-permute-start.2
  28.4 5.1 %collective-permute-done.4.refs_3_ = bf16[2,128,256]{2,1,0:T(8,128)(2,1)S(1)} collective-permute-done((bf16[2,128,256]{2,1,0:T(8,128)(2,1)S(1)}, bf16[2,128,256]{2,1,0:T(8,128)(2,1)S(1)}, u32[]{:S(2)}, u32[]{:S(2)}) %collective-permute-start.4) | collective-permute-done | bytes 131104 | tf_op jit(solution)/shard_map/ppermute | solution.py:19
  33.5 0.0 collective-permute-done.3.refs_2_
  33.5 3.3 %collective-permute-done.2.refs_1_ = bf16[2,128,256]{2,1,0:T(8,128)(2,1)S(1)} collective-permute-done((bf16[2,128,256]{2,1,0:T(8,128)(2,1)S(1)}, bf16[2,128,256]{2,1,0:T(8,128)(2,1)S(1)}, u32[]{:S(2)}, u32[]{:S(2)}) %collective-permute-start.2) | collective-permute-done | bytes 131104 | tf_op jit(solution)/shard_map/ppermute | solution.py:19
  36.8 1.6 %predict.1 = (f32[128,512]{1,0:T(8,128)S(1)}, s16[144,512]{1,0:T(8,128)(2,1)S(1)}, s16[144,512]{1,0:T(8,128)(2,1)S(1)}, s16[144,512]{1,0:T(8,128)(2,1)S(1)}, bf1...) custom-call(s32[5]{0:T(128)S(1)} %stack.23.place.refs_0_, ...), custom_call_target="tpu_custom_call" | custom-call | tf_op jit(solution)/shard_map/predict/pallas_call | solution.py:190
  38.4 0.0 copy-start.3
  38.4 0.1 collective-permute-start.12
  38.5 0.1 collective-permute-start.13
  38.6 2.6 %collective-permute-start.14 = (s16[144,512]{1,0:T(8,128)(2,1)S(1)}, s16[144,512]{1,0:T(8,128)(2,1)S(1)}, u32[]{:S(2)}, u32[]{:S(2)}) collective-permute-start(s16[144,512]{1,0:T(8,128)(2,1)S(1)} %get-tuple-element.32), channel_id=1, source_target_pairs={{0,192},{64,0},{128,64},{192,128},{1,193},{65,1},{129,65},{193,129... | collective-permute-start | bytes 442376 | tf_op jit(solution)/shard_map/ppermute | solution.py:19
  41.1 6.6 %collective-permute-done.12.p1 = s16[144,512]{1,0:T(8,128)(2,1)S(1)} collective-permute-done((s16[144,512]{1,0:T(8,128)(2,1)S(1)}, s16[144,512]{1,0:T(8,128)(2,1)S(1)}, u32[]{:S(2)}, u32[]{:S(2)}) %collective-permute-start.12) | collective-permute-done | bytes 147488 | tf_op jit(solution)/shard_map/ppermute | solution.py:19
  47.7 0.0 collective-permute-done.13.p2
  47.7 0.0 collective-permute-done.14.p3
  47.7 1.4 %residual.1 = (f32[2,64,512]{2,1,0:T(8,128)}, s16[144,512]{1,0:T(8,128)(2,1)S(1)}) custom-call(s32[5]{0:T(128)S(1)} %stack.23.place.refs_0_, f32[128,512]{1,0:T(8,128)S(1)} %get-tuple-element.29.p0, s16[144,512]{1,0:T(8,128)(2,1)S(1)} %collective-permute-done.12.p1, s16[144,512]{1,0:T(8,128)(2,1)S(1)} %collective-permute-done.13.p2, ...), custom_call_target="tpu_custom_call" | custom-call | tf_op jit(solution)/shard_map/residual/pallas_call | solution.py:198
  49.2 3.2 %collective-permute-start.17 = (s16[144,512]{1,0:T(8,128)(2,1)S(1)}, s16[144,512]{1,0:T(8,128)(2,1)S(1)}, u32[]{:S(2)}, u32[]{:S(2)}) collective-permute-start(s16[144,512]{1,0:T(8,128)(2,1)S(1)} %get-tuple-element.36.e0), channel_id=1, source_target_pairs={{0,192},{64,0},{128,64},{192,128},{1,193},{65,1},{129,65},{193,129... | collective-permute-start | bytes 442376 | tf_op jit(solution)/shard_map/ppermute | solution.py:19
  52.3 0.0 collective-permute-start.16
  52.3 0.6 collective-permute-start.15
  52.9 5.3 %collective-permute-done.17.e3 = s16[144,512]{1,0:T(8,128)(2,1)S(1)} collective-permute-done((s16[144,512]{1,0:T(8,128)(2,1)S(1)}, s16[144,512]{1,0:T(8,128)(2,1)S(1)}, u32[]{:S(2)}, u32[]{:S(2)}) %collective-permute-start.17) | collective-permute-done | bytes 147488 | tf_op jit(solution)/shard_map/ppermute | solution.py:19
  58.3 3.9 %collective-permute-done.15.e1 = s16[144,512]{1,0:T(8,128)(2,1)S(1)} collective-permute-done((s16[144,512]{1,0:T(8,128)(2,1)S(1)}, s16[144,512]{1,0:T(8,128)(2,1)S(1)}, u32[]{:S(2)}, u32[]{:S(2)}) %collective-permute-start.15) | collective-permute-done | bytes 147488 | tf_op jit(solution)/shard_map/ppermute | solution.py:19
  62.1 3.4 %grads.1 = (f32[128,512]{1,0:T(8,128)S(1)}, f32[128,512]{1,0:T(8,128)S(1)}, f32[128,512]{1,0:T(8,128)S(1)}, s16[2,144,512]{2,1,0:T(8,128)(2,1)S(1)}, s16[2,144,5...) custom-call(s32[5]{0:T(128)S(1)} %stack.23.place.refs_0_, ...), custom_call_target="tpu_custom_call" | custom-call | tf_op jit(solution)/shard_map/grads/pallas_call | solution.py:202
  65.5 0.9 collective-permute-start.18
  66.4 0.2 collective-permute-start.22
  66.6 2.5 %collective-permute-start.23 = (s16[2,144,512]{2,1,0:T(8,128)(2,1)S(1)}, s16[2,144,512]{2,1,0:T(8,128)(2,1)S(1)}, u32[]{:S(2)}, u32[]{:S(2)}) collective-permute-start(s16[2,144,512]{2,1,0:T(8,128)(2,1)S(1)} %get-tuple-element.45), channel_id=1, source_target_pairs={{0,56},{8,0},{16,8},{24,16},{32,24},{40,32},{48,40},{56,48},{1,57}... | collective-permute-start | bytes 884744 | tf_op jit(solution)/shard_map/ppermute | solution.py:19
  69.1 0.6 core_sum.1
  69.7 0.1 collective-permute-start.19
  69.8 1.0 %collective-permute-start.20 = (f32[128,256]{1,0:T(8,128)S(1)}, f32[128,256]{1,0:T(8,128)S(1)}, u32[]{:S(2)}, u32[]{:S(2)}) collective-permute-start(f32[128,256]{1,0:T(8,128)S(1)} %get-tuple-element.41), channel_id=1, source_target_pairs={{0,4},{2,6},{4,0},{6,2},{1,5},{3,7},{5,1},{7,3},{8,12},{10,14},{12... | collective-permute-start | bytes 393224 | tf_op jit(solution)/shard_map/ppermute | solution.py:19
  70.9 1.6 %collective-permute-start.21 = (f32[128,256]{1,0:T(8,128)S(1)}, f32[128,256]{1,0:T(8,128)S(1)}, u32[]{:S(2)}, u32[]{:S(2)}) collective-permute-start(f32[128,256]{1,0:T(8,128)S(1)} %get-tuple-element.42), channel_id=1, source_target_pairs={{0,6},{2,0},{4,2},{6,4},{1,7},{3,1},{5,3},{7,5},{8,14},{10,8},{12,... | collective-permute-start | bytes 393224 | tf_op jit(solution)/shard_map/ppermute | solution.py:19
  72.5 3.7 %collective-permute-done.22.up = s16[2,144,512]{2,1,0:T(8,128)(2,1)S(1)} collective-permute-done((s16[2,144,512]{2,1,0:T(8,128)(2,1)S(1)}, s16[2,144,512]{2,1,0:T(8,128)(2,1)S(1)}, u32[]{:S(2)}, u32[]{:S(2)}) %collective-permute-start.22) | collective-permute-done | bytes 294944 | tf_op jit(solution)/shard_map/ppermute | solution.py:19
  76.2 1.8 %collective-permute-start.26 = (s16[144,512]{1,0:T(8,128)(2,1)S(1)}, s16[144,512]{1,0:T(8,128)(2,1)S(1)}, u32[]{:S(2)}, u32[]{:S(2)}) collective-permute-start(s16[144,512]{1,0:T(8,128)(2,1)S(1)} %get-tuple-element.51), channel_id=1, source_target_pairs={{0,32},{8,40},{16,48},{24,56},{32,0},{40,8},{48,16},{56,24},{1,33}... | collective-permute-start | bytes 442376 | tf_op jit(solution)/shard_map/ppermute | solution.py:19
  78.0 0.0 collective-permute-done.23.down
  78.0 0.7 relay.1
  78.7 1.9 %collective-permute-start.24 = (s16[144,512]{1,0:T(8,128)(2,1)S(1)}, s16[144,512]{1,0:T(8,128)(2,1)S(1)}, u32[]{:S(2)}, u32[]{:S(2)}) collective-permute-start(s16[144,512]{1,0:T(8,128)(2,1)S(1)} %get-tuple-element.49), channel_id=1, source_target_pairs={{0,16},{8,24},{16,32},{24,40},{32,48},{40,56},{48,0},{56,8},{1,17}... | collective-permute-start | bytes 442376 | tf_op jit(solution)/shard_map/ppermute | solution.py:19
  80.6 0.0 collective-permute-done.19.s1
  80.6 1.7 %collective-permute-start.25 = (s16[144,512]{1,0:T(8,128)(2,1)S(1)}, s16[144,512]{1,0:T(8,128)(2,1)S(1)}, u32[]{:S(2)}, u32[]{:S(2)}) collective-permute-start(s16[144,512]{1,0:T(8,128)(2,1)S(1)} %get-tuple-element.50), channel_id=1, source_target_pairs={{0,48},{8,56},{16,0},{24,8},{32,16},{40,24},{48,32},{56,40},{1,49}... | collective-permute-start | bytes 442376 | tf_op jit(solution)/shard_map/ppermute | solution.py:19
  82.4 0.0 collective-permute-done.20.s2
  82.4 0.0 collective-permute-done.21.s3
  82.4 0.6 refl_sum.1
  83.0 0.7 collective-permute-start.27
  83.7 3.6 %collective-permute-done.26.refs_4_ = s16[144,512]{1,0:T(8,128)(2,1)S(1)} collective-permute-done((s16[144,512]{1,0:T(8,128)(2,1)S(1)}, s16[144,512]{1,0:T(8,128)(2,1)S(1)}, u32[]{:S(2)}, u32[]{:S(2)}) %collective-permute-start.26) | collective-permute-done | bytes 147488 | tf_op jit(solution)/shard_map/ppermute | solution.py:19
  87.3 1.5 %collective-permute-done.24.refs_2_ = s16[144,512]{1,0:T(8,128)(2,1)S(1)} collective-permute-done((s16[144,512]{1,0:T(8,128)(2,1)S(1)}, s16[144,512]{1,0:T(8,128)(2,1)S(1)}, u32[]{:S(2)}, u32[]{:S(2)}) %collective-permute-start.24) | collective-permute-done | bytes 147488 | tf_op jit(solution)/shard_map/ppermute | solution.py:19
  88.8 5.3 %collective-permute-done.25.refs_3_ = s16[144,512]{1,0:T(8,128)(2,1)S(1)} collective-permute-done((s16[144,512]{1,0:T(8,128)(2,1)S(1)}, s16[144,512]{1,0:T(8,128)(2,1)S(1)}, u32[]{:S(2)}, u32[]{:S(2)}) %collective-permute-start.25) | collective-permute-done | bytes 147488 | tf_op jit(solution)/shard_map/ppermute | solution.py:19
  94.1 0.0 collective-permute-done.27.refs_5_
  94.1 1.4 %last.1 = (f32[2,64,512]{2,1,0:T(8,128)}, f32[2,64,256]{2,1,0:T(8,128)}) custom-call(s32[5]{0:T(128)S(1)} %stack.23.place.refs_0_, f32[128,512]{1,0:T(8,128)S(1)} %get-tuple-element.46.refs_1_, s16[144,512]{1,0:T(8,128)(2,1)S(1)} %collective-permute-done.24.refs_2_, s16[144,512]{1,0:T(8,128)(2,1)S(1)} %collective-permute-done.25.refs_3_, ...), custom_call_target="tpu_custom_call" | custom-call | tf_op jit(solution)/shard_map/last/pallas_call | solution.py:231
  (9 shorter events, 0.0 us)
Async XLA Ops:
  0.6 12.3 %collective-permute-start.9 = (bf16[2,64,512]{2,1,0:T(8,128)(2,1)}, bf16[2,64,512]{2,1,0:T(8,128)(2,1)S(1)}, u32[]{:S(2)}, u32[]{:S(2)}) collective-permute-start(bf16[2,64,512]{2,1,0:T(8,128)(2,1)} %bitcast.17), channel_id=1, source_target_pairs={{0,48},{8,56},{16,0},{24,8},{32,16},{40,24},{48,32},{56,40},{1,49}... | collective-permute-start | bytes 393224 | tf_op jit(solution)/shard_map/ppermute | solution.py:19
  7.6 3.0 %collective-permute-start = (bf16[2,64,256]{2,1,0:T(8,128)(2,1)}, bf16[2,64,256]{2,1,0:T(8,128)(2,1)S(1)}, u32[]{:S(2)}, u32[]{:S(2)}) collective-permute-start(bf16[2,64,256]{2,1,0:T(8,128)(2,1)} %bitcast.23), channel_id=1, source_target_pairs={{0,1},{1,0},{2,3},{3,2},{4,5},{5,4},{6,7},{7,6},{8,9},{9,8},{10,11... | collective-permute-start | bytes 196616 | tf_op jit(solution)/shard_map/ppermute | solution.py:19
  8.5 11.0 %collective-permute-start.11 = (bf16[2,64,512]{2,1,0:T(8,128)(2,1)}, bf16[2,64,512]{2,1,0:T(8,128)(2,1)S(1)}, u32[]{:S(2)}, u32[]{:S(2)}) collective-permute-start(bf16[2,64,512]{2,1,0:T(8,128)(2,1)} %bitcast.18), channel_id=1, source_target_pairs={{0,56},{8,0},{16,8},{24,16},{32,24},{40,32},{48,40},{56,48},{1,57}... | collective-permute-start | bytes 393224 | tf_op jit(solution)/shard_map/ppermute | solution.py:19
  9.2 10.3 %collective-permute-start.6 = (bf16[2,64,512]{2,1,0:T(8,128)(2,1)}, bf16[2,64,512]{2,1,0:T(8,128)(2,1)S(1)}, u32[]{:S(2)}, u32[]{:S(2)}) collective-permute-start(bf16[2,64,512]{2,1,0:T(8,128)(2,1)} %bitcast.19), channel_id=1, source_target_pairs={{0,16},{8,24},{16,32},{24,40},{32,48},{40,56},{48,0},{56,8},{1,17}... | collective-permute-start | bytes 393224 | tf_op jit(solution)/shard_map/ppermute | solution.py:19
  10.5 2.3 %copy-start = (bf16[2,1,64,512]{3,2,1,0:T(8,128)(2,1)S(1)}, bf16[2,1,64,512]{3,2,1,0:T(8,128)(2,1)}, u32[]{:S(2)}) copy-start(bf16[2,1,64,512]{3,2,1,0:T(8,128)(2,1)} %param.5) | copy-start | bytes 393220
  10.5 0.9 copy-start.2
  12.0 35.8 %copy-start.1 = (bf16[2,1,64,512]{3,2,1,0:T(8,128)(2,1)S(1)}, bf16[2,1,64,512]{3,2,1,0:T(8,128)(2,1)}, u32[]{:S(2)}) copy-start(bf16[2,1,64,512]{3,2,1,0:T(8,128)(2,1)} %param.6) | copy-start | bytes 393220
  12.0 7.6 %collective-permute-start.1 = (bf16[2,128,256]{2,1,0:T(8,128)(2,1)S(1)}, bf16[2,128,256]{2,1,0:T(8,128)(2,1)S(1)}, u32[]{:S(2)}, u32[]{:S(2)}) collective-permute-start(bf16[2,128,256]{2,1,0:T(8,128)(2,1)S(1)} %pair.1), channel_id=1, source_target_pairs={{0,0},{2,64},{4,128},{6,192},{64,2},{66,66},{68,130},{70,194},{128... | collective-permute-start | bytes 393224 | tf_op jit(solution)/shard_map/ppermute | solution.py:24
  12.8 15.0 %collective-permute-start.5 = (bf16[2,64,512]{2,1,0:T(8,128)(2,1)S(1)}, bf16[2,64,512]{2,1,0:T(8,128)(2,1)S(1)}, u32[]{:S(2)}, u32[]{:S(2)}) collective-permute-start(bf16[2,64,512]{2,1,0:T(8,128)(2,1)S(1)} %bitcast.20), channel_id=1, source_target_pairs={{0,8},{8,16},{16,24},{24,32},{32,40},{40,48},{48,56},{56,0},{1,9},... | collective-permute-start | bytes 393224 | tf_op jit(solution)/shard_map/ppermute | solution.py:19
  12.9 14.9 %collective-permute-start.10 = (bf16[2,64,512]{2,1,0:T(8,128)(2,1)S(1)}, bf16[2,64,512]{2,1,0:T(8,128)(2,1)S(1)}, u32[]{:S(2)}, u32[]{:S(2)}) collective-permute-start(bf16[2,64,512]{2,1,0:T(8,128)(2,1)S(1)} %collective-permute-done.9.refs_10_), channel_id=1, source_target_pairs={{0,56},{8,0},{16,8},{24,16},{32,24},{40,32},{48,40},{56,48},{1,57}... | collective-permute-start | bytes 393224 | tf_op jit(solution)/shard_map/ppermute | solution.py:19
  19.5 8.9 %collective-permute-start.8 = (bf16[2,64,512]{2,1,0:T(8,128)(2,1)S(1)}, bf16[2,64,512]{2,1,0:T(8,128)(2,1)S(1)}, u32[]{:S(2)}, u32[]{:S(2)}) collective-permute-start(bf16[2,64,512]{2,1,0:T(8,128)(2,1)S(1)} %collective-permute-done.6.refs_6_), channel_id=1, source_target_pairs={{0,16},{8,24},{16,32},{24,40},{32,48},{40,56},{48,0},{56,8},{1,17}... | collective-permute-start | bytes 393224 | tf_op jit(solution)/shard_map/ppermute | solution.py:19
  19.5 8.8 %collective-permute-start.7 = (bf16[2,64,512]{2,1,0:T(8,128)(2,1)S(1)}, bf16[2,64,512]{2,1,0:T(8,128)(2,1)S(1)}, u32[]{:S(2)}, u32[]{:S(2)}) collective-permute-start(bf16[2,64,512]{2,1,0:T(8,128)(2,1)S(1)} %collective-permute-done.6.refs_6_), channel_id=1, source_target_pairs={{0,8},{8,16},{16,24},{24,32},{32,40},{40,48},{48,56},{56,0},{1,9},... | collective-permute-start | bytes 393224 | tf_op jit(solution)/shard_map/ppermute | solution.py:19
  19.6 13.9 %collective-permute-start.4 = (bf16[2,128,256]{2,1,0:T(8,128)(2,1)S(1)}, bf16[2,128,256]{2,1,0:T(8,128)(2,1)S(1)}, u32[]{:S(2)}, u32[]{:S(2)}) collective-permute-start(bf16[2,128,256]{2,1,0:T(8,128)(2,1)S(1)} %collective-permute-done.1.refs_0_), channel_id=1, source_target_pairs={{0,6},{2,0},{4,2},{6,4},{1,7},{3,1},{5,3},{7,5},{8,14},{10,8},{12,... | collective-permute-start | bytes 393224 | tf_op jit(solution)/shard_map/ppermute | solution.py:19
  27.8 5.7 %collective-permute-start.3 = (bf16[2,128,256]{2,1,0:T(8,128)(2,1)S(1)}, bf16[2,128,256]{2,1,0:T(8,128)(2,1)S(1)}, u32[]{:S(2)}, u32[]{:S(2)}) collective-permute-start(bf16[2,128,256]{2,1,0:T(8,128)(2,1)S(1)} %collective-permute-done.1.refs_0_), channel_id=1, source_target_pairs={{0,4},{2,6},{4,0},{6,2},{1,5},{3,7},{5,1},{7,3},{8,12},{10,14},{12... | collective-permute-start | bytes 393224 | tf_op jit(solution)/shard_map/ppermute | solution.py:19
  27.8 9.0 %collective-permute-start.2 = (bf16[2,128,256]{2,1,0:T(8,128)(2,1)S(1)}, bf16[2,128,256]{2,1,0:T(8,128)(2,1)S(1)}, u32[]{:S(2)}, u32[]{:S(2)}) collective-permute-start(bf16[2,128,256]{2,1,0:T(8,128)(2,1)S(1)} %collective-permute-done.1.refs_0_), channel_id=1, source_target_pairs={{0,2},{2,4},{4,6},{6,0},{1,3},{3,5},{5,7},{7,1},{8,10},{10,12},{12... | collective-permute-start | bytes 393224 | tf_op jit(solution)/shard_map/ppermute | solution.py:19
  38.4 9.4 %copy-start.3 = (s32[8,20]{1,0:T(8,128)S(1)}, s32[8,20]{1,0:T(8,128)}, u32[]{:S(2)}) copy-start(s32[8,20]{1,0:T(8,128)} %rec.1) | copy-start | bytes 1924
  38.4 9.3 %collective-permute-start.12 = (s16[144,512]{1,0:T(8,128)(2,1)S(1)}, s16[144,512]{1,0:T(8,128)(2,1)S(1)}, u32[]{:S(2)}, u32[]{:S(2)}) collective-permute-start(s16[144,512]{1,0:T(8,128)(2,1)S(1)} %get-tuple-element.30), channel_id=1, source_target_pairs={{0,64},{64,128},{128,192},{192,0},{1,65},{65,129},{129,193},{193,1... | collective-permute-start | bytes 442376 | tf_op jit(solution)/shard_map/ppermute | solution.py:19
  38.5 9.2 %collective-permute-start.13 = (s16[144,512]{1,0:T(8,128)(2,1)S(1)}, s16[144,512]{1,0:T(8,128)(2,1)S(1)}, u32[]{:S(2)}, u32[]{:S(2)}) collective-permute-start(s16[144,512]{1,0:T(8,128)(2,1)S(1)} %get-tuple-element.31), channel_id=1, source_target_pairs={{0,128},{64,192},{128,0},{192,64},{1,129},{65,193},{129,1},{193,65... | collective-permute-start | bytes 442376 | tf_op jit(solution)/shard_map/ppermute | solution.py:19
  38.6 9.1 %collective-permute-start.14 = (s16[144,512]{1,0:T(8,128)(2,1)S(1)}, s16[144,512]{1,0:T(8,128)(2,1)S(1)}, u32[]{:S(2)}, u32[]{:S(2)}) collective-permute-start(s16[144,512]{1,0:T(8,128)(2,1)S(1)} %get-tuple-element.32), channel_id=1, source_target_pairs={{0,192},{64,0},{128,64},{192,128},{1,193},{65,1},{129,65},{193,129... | collective-permute-start | bytes 442376 | tf_op jit(solution)/shard_map/ppermute | solution.py:19
  49.2 9.1 %collective-permute-start.17 = (s16[144,512]{1,0:T(8,128)(2,1)S(1)}, s16[144,512]{1,0:T(8,128)(2,1)S(1)}, u32[]{:S(2)}, u32[]{:S(2)}) collective-permute-start(s16[144,512]{1,0:T(8,128)(2,1)S(1)} %get-tuple-element.36.e0), channel_id=1, source_target_pairs={{0,192},{64,0},{128,64},{192,128},{1,193},{65,1},{129,65},{193,129... | collective-permute-start | bytes 442376 | tf_op jit(solution)/shard_map/ppermute | solution.py:19
  52.3 5.9 %collective-permute-start.16 = (s16[144,512]{1,0:T(8,128)(2,1)S(1)}, s16[144,512]{1,0:T(8,128)(2,1)S(1)}, u32[]{:S(2)}, u32[]{:S(2)}) collective-permute-start(s16[144,512]{1,0:T(8,128)(2,1)S(1)} %get-tuple-element.36.e0), channel_id=1, source_target_pairs={{0,128},{64,192},{128,0},{192,64},{1,129},{65,193},{129,1},{193,65... | collective-permute-start | bytes 442376 | tf_op jit(solution)/shard_map/ppermute | solution.py:19
  52.3 9.8 %collective-permute-start.15 = (s16[144,512]{1,0:T(8,128)(2,1)S(1)}, s16[144,512]{1,0:T(8,128)(2,1)S(1)}, u32[]{:S(2)}, u32[]{:S(2)}) collective-permute-start(s16[144,512]{1,0:T(8,128)(2,1)S(1)} %get-tuple-element.36.e0), channel_id=1, source_target_pairs={{0,64},{64,128},{128,192},{192,0},{1,65},{65,129},{129,193},{193,1... | collective-permute-start | bytes 442376 | tf_op jit(solution)/shard_map/ppermute | solution.py:19
  65.5 3.6 %collective-permute-start.18 = (f32[4,128,256]{2,1,0:T(8,128)S(1)}, f32[4,128,256]{2,1,0:T(8,128)S(1)}, u32[]{:S(2)}, u32[]{:S(2)}) collective-permute-start(f32[4,128,256]{2,1,0:T(8,128)S(1)} %get-tuple-element.38), channel_id=1, source_target_pairs={{0,1},{1,0},{2,3},{3,2},{4,5},{5,4},{6,7},{7,6},{8,9},{9,8},{10,11... | collective-permute-start | bytes 1572872 | tf_op jit(solution)/shard_map/ppermute | solution.py:19
  66.4 9.8 %collective-permute-start.22 = (s16[2,144,512]{2,1,0:T(8,128)(2,1)S(1)}, s16[2,144,512]{2,1,0:T(8,128)(2,1)S(1)}, u32[]{:S(2)}, u32[]{:S(2)}) collective-permute-start(s16[2,144,512]{2,1,0:T(8,128)(2,1)S(1)} %get-tuple-element.44), channel_id=1, source_target_pairs={{0,8},{8,16},{16,24},{24,32},{32,40},{40,48},{48,56},{56,0},{1,9},... | collective-permute-start | bytes 884744 | tf_op jit(solution)/shard_map/ppermute | solution.py:19
  66.6 11.3 %collective-permute-start.23 = (s16[2,144,512]{2,1,0:T(8,128)(2,1)S(1)}, s16[2,144,512]{2,1,0:T(8,128)(2,1)S(1)}, u32[]{:S(2)}, u32[]{:S(2)}) collective-permute-start(s16[2,144,512]{2,1,0:T(8,128)(2,1)S(1)} %get-tuple-element.45), channel_id=1, source_target_pairs={{0,56},{8,0},{16,8},{24,16},{32,24},{40,32},{48,40},{56,48},{1,57}... | collective-permute-start | bytes 884744 | tf_op jit(solution)/shard_map/ppermute | solution.py:19
  69.7 10.9 %collective-permute-start.19 = (f32[128,256]{1,0:T(8,128)S(1)}, f32[128,256]{1,0:T(8,128)S(1)}, u32[]{:S(2)}, u32[]{:S(2)}) collective-permute-start(f32[128,256]{1,0:T(8,128)S(1)} %get-tuple-element.40), channel_id=1, source_target_pairs={{0,2},{2,4},{4,6},{6,0},{1,3},{3,5},{5,7},{7,1},{8,10},{10,12},{12... | collective-permute-start | bytes 393224 | tf_op jit(solution)/shard_map/ppermute | solution.py:19
  69.8 12.5 %collective-permute-start.20 = (f32[128,256]{1,0:T(8,128)S(1)}, f32[128,256]{1,0:T(8,128)S(1)}, u32[]{:S(2)}, u32[]{:S(2)}) collective-permute-start(f32[128,256]{1,0:T(8,128)S(1)} %get-tuple-element.41), channel_id=1, source_target_pairs={{0,4},{2,6},{4,0},{6,2},{1,5},{3,7},{5,1},{7,3},{8,12},{10,14},{12... | collective-permute-start | bytes 393224 | tf_op jit(solution)/shard_map/ppermute | solution.py:19
  70.9 11.5 %collective-permute-start.21 = (f32[128,256]{1,0:T(8,128)S(1)}, f32[128,256]{1,0:T(8,128)S(1)}, u32[]{:S(2)}, u32[]{:S(2)}) collective-permute-start(f32[128,256]{1,0:T(8,128)S(1)} %get-tuple-element.42), channel_id=1, source_target_pairs={{0,6},{2,0},{4,2},{6,4},{1,7},{3,1},{5,3},{7,5},{8,14},{10,8},{12,... | collective-permute-start | bytes 393224 | tf_op jit(solution)/shard_map/ppermute | solution.py:19
  76.2 11.1 %collective-permute-start.26 = (s16[144,512]{1,0:T(8,128)(2,1)S(1)}, s16[144,512]{1,0:T(8,128)(2,1)S(1)}, u32[]{:S(2)}, u32[]{:S(2)}) collective-permute-start(s16[144,512]{1,0:T(8,128)(2,1)S(1)} %get-tuple-element.51), channel_id=1, source_target_pairs={{0,32},{8,40},{16,48},{24,56},{32,0},{40,8},{48,16},{56,24},{1,33}... | collective-permute-start | bytes 442376 | tf_op jit(solution)/shard_map/ppermute | solution.py:19
  78.7 10.1 %collective-permute-start.24 = (s16[144,512]{1,0:T(8,128)(2,1)S(1)}, s16[144,512]{1,0:T(8,128)(2,1)S(1)}, u32[]{:S(2)}, u32[]{:S(2)}) collective-permute-start(s16[144,512]{1,0:T(8,128)(2,1)S(1)} %get-tuple-element.49), channel_id=1, source_target_pairs={{0,16},{8,24},{16,32},{24,40},{32,48},{40,56},{48,0},{56,8},{1,17}... | collective-permute-start | bytes 442376 | tf_op jit(solution)/shard_map/ppermute | solution.py:19
  80.6 13.4 %collective-permute-start.25 = (s16[144,512]{1,0:T(8,128)(2,1)S(1)}, s16[144,512]{1,0:T(8,128)(2,1)S(1)}, u32[]{:S(2)}, u32[]{:S(2)}) collective-permute-start(s16[144,512]{1,0:T(8,128)(2,1)S(1)} %get-tuple-element.50), channel_id=1, source_target_pairs={{0,48},{8,56},{16,0},{24,8},{32,16},{40,24},{48,32},{56,40},{1,49}... | collective-permute-start | bytes 442376 | tf_op jit(solution)/shard_map/ppermute | solution.py:19
  83.0 11.0 %collective-permute-start.27 = (f32[128,256]{1,0:T(8,128)S(1)}, f32[128,256]{1,0:T(8,128)S(1)}, u32[]{:S(2)}, u32[]{:S(2)}) collective-permute-start(f32[128,256]{1,0:T(8,128)S(1)} %get-tuple-element.52), channel_id=1, source_target_pairs={{0,0},{2,64},{4,128},{6,192},{64,2},{66,66},{68,130},{70,194},{128... | collective-permute-start | bytes 393224 | tf_op jit(solution)/shard_map/ppermute | solution.py:24
where the time goes:
time: 95.6 us; the launch traced here: 95.5 us
  waiting for transfers between devices  41.8 us (44%)
  starting transfers between devices  41.6 us (44%)
  Pallas kernels  10.3 us (11%)
  local copies, waits for them, and re-layouts  0.98 us (1%)
    ppermute x26, waiting for transfers between devices, send(): lax.ppermute(value, axis, [(i, (i + step) % size) for i in range(size)])  41.8 us
    ppermute x26, starting transfers between devices, send(): lax.ppermute(value, axis, [(i, (i + step) % size) for i in range(size)])  40.1 us
    pallas_call x1, Pallas kernels, shards(): kernel_call(grads_kernel, [((128, 512), F32)] * 3 + [((2, 144, 512), I16)...  3.36 us
  transfers between devices with their start and end apart: 28, of which 10 were waited for; matrix products, arithmetic and copies ran while one was open for 0% of the time, Pallas kernels for 3%

commit v1 on v0

--- a/solution.py
+++ b/solution.py
@@ -92,6 +92,28 @@
     return coded[0:rows, :].astype(jnp.int32).astype(F32) * scale
 
 
+def scaled(value):
+    most = jnp.max(jnp.abs(value), axis=0, keepdims=True)
+    code = jnp.ceil(jnp.log2(jnp.maximum(most, 2.0**-100)) * 128.0 + 0.01)
+    number = value * (jnp.exp2(code * (-1.0 / 128.0)) * 32767.0)
+    return jnp.clip(jnp.round(number), -32767.0, 32767.0), code
+
+
+def encode_pair(first, second, out):
+    codes = []
+    for i, value in enumerate((first, second)):
+        number, code = scaled(value)
+        out[128 * i : 128 * i + 128, :] = number.astype(jnp.int32).astype(jnp.int16)
+        codes.append(jnp.broadcast_to(code, (8, value.shape[1])))
+    out[256:272, :] = jnp.concatenate(codes, axis=0).astype(jnp.int32).astype(jnp.int16)
+
+
+def decode_pair(coded, i):
+    code = coded[256:272, :].astype(jnp.int32).astype(F32)[8 * i : 8 * i + 1]
+    scale = jnp.exp2(code * (1.0 / 128.0)) * (1.0 / 32767.0)
+    return coded[128 * i : 128 * i + 128, :].astype(jnp.int32).astype(F32) * scale
+
+
 def grads_kernel(place, refl, wave, e0, e1, e2, e3, here, two, back, up, down, far, own, other, high, low, sums):
     mx, mc = place[0], place[2]
     for k, e in enumerate((e0, e1, e2, e3)):
@@ -120,10 +142,8 @@
     here[...] = toward(0)
     two[...] = toward(2)
     back[...] = toward(-2)
-    encode(toward(1), up.at[0])
-    encode(toward(3), up.at[1])
-    encode(toward(-1), down.at[0])
-    encode(toward(-3), down.at[1])
+    encode_pair(toward(1), toward(3), up)
+    encode_pair(toward(-1), toward(-3), down)
     encode(toward(4), far)
     for to, half in ((own, mc), (other, 1 - mc)):
         w = wave[pl.ds(4 * half, 4)].reshape(256, 1024)
@@ -141,12 +161,12 @@
 
 def refl_sum_kernel(place, s0, s1, s2, s3, here, up, down, out, base):
     out[...] = (s0[...] + s1[...]) + (s2[...] + s3[...])
-    base[...] = here[...] + decode(up.at[0]) + decode(down.at[0])
+    base[...] = here[...] + decode_pair(up, 0) + decode_pair(down, 0)
 
 
 def relay_kernel(place, two, back, up, down, after, out_up, out_down):
-    encode(two[...] + decode(up.at[1]), out_up)
-    encode(back[...] + decode(down.at[1]), out_down)
+    encode(two[...] + decode_pair(up, 1), out_up)
+    encode(back[...] + decode_pair(down, 1), out_down)
 
 
 def last_kernel(scale, refl_scale, place, base, up2, down2, far, grad, out, refl_out):
@@ -202,7 +222,7 @@
     here, two, back, up, down, far, own, other = kernel_call(
         grads_kernel,
         [((128, 512), F32)] * 3
-        + [((2, 144, 512), I16)] * 2
+        + [((272, 512), I16)] * 2
         + [((144, 512), I16)]
         + [((X, 128, 256), F32)] * 2,
         [VMEM] * 6,

time: 95.6 us -> 95.3 us (level)
  no operation moved by 1% of the time
where the time goes in v1:
time: 95.3 us; the launch traced here: 95.1 us
  starting transfers between devices  41.6 us (44%)
  waiting for transfers between devices  41.5 us (44%)
  Pallas kernels  10.3 us (11%)
  local copies, waits for them, and re-layouts  0.98 us (1%)
    ppermute x26, waiting for transfers between devices, send(): lax.ppermute(value, axis, [(i, (i + step) % size) for i in range(size)])  41.5 us
    ppermute x26, starting transfers between devices, send(): lax.ppermute(value, axis, [(i, (i + step) % size) for i in range(size)])  40.1 us
    pallas_call x1, Pallas kernels, shards(): kernel_call(grads_kernel, [((128, 512), F32)] * 3 + [((272, 512), I16)] *...  3.36 us
  transfers between devices with their start and end apart: 28, of which 10 were waited for; matrix products, arithmetic and copies ran while one was open for 0% of the time, Pallas kernels for 3%

profile of v1, /device:TPU:1, one launch (start us, length us, event | category | flops | bytes accessed | tf_op | source)
XLA Modules:
  0.0 95.1 jit_solution(1854404429227383604)
XLA Ops:
  0.6 6.9 %collective-permute-start.9 = (bf16[2,64,512]{2,1,0:T(8,128)(2,1)}, bf16[2,64,512]{2,1,0:T(8,128)(2,1)S(1)}, u32[]{:S(2)}, u32[]{:S(2)}) collective-permute-start(bf16[2,64,512]{2,1,0:T(8,128)(2,1)} %bitcast.17), channel_id=1, source_target_pairs={{0,48},{8,56},{16,0},{24,8},{32,16},{40,24},{48,32},{56,40},{1,49}... | collective-permute-start | bytes 393224 | tf_op jit(solution)/shard_map/ppermute | solution.py:19
  7.6 1.0 %collective-permute-start = (bf16[2,64,256]{2,1,0:T(8,128)(2,1)}, bf16[2,64,256]{2,1,0:T(8,128)(2,1)S(1)}, u32[]{:S(2)}, u32[]{:S(2)}) collective-permute-start(bf16[2,64,256]{2,1,0:T(8,128)(2,1)} %bitcast.23), channel_id=1, source_target_pairs={{0,1},{1,0},{2,3},{3,2},{4,5},{5,4},{6,7},{7,6},{8,9},{9,8},{10,11... | collective-permute-start | bytes 196616 | tf_op jit(solution)/shard_map/ppermute | solution.py:19
  8.5 0.7 collective-permute-start.11
  9.2 1.2 %collective-permute-start.6 = (bf16[2,64,512]{2,1,0:T(8,128)(2,1)}, bf16[2,64,512]{2,1,0:T(8,128)(2,1)S(1)}, u32[]{:S(2)}, u32[]{:S(2)}) collective-permute-start(bf16[2,64,512]{2,1,0:T(8,128)(2,1)} %bitcast.19), channel_id=1, source_target_pairs={{0,16},{8,24},{16,32},{24,40},{32,48},{40,56},{48,0},{56,8},{1,17}... | collective-permute-start | bytes 393224 | tf_op jit(solution)/shard_map/ppermute | solution.py:19
  10.4 0.1 stack.23.place.refs_0_
  10.5 0.0 collective-permute-done.theirs
  10.5 0.9 copy-done.2
  11.4 0.6 pair.1
  12.0 0.0 copy-start.1
  12.0 0.8 collective-permute-start.1
  12.8 0.1 collective-permute-start.5
  12.9 0.0 collective-permute-done.9.refs_10_
  12.9 3.1 %collective-permute-start.10 = (bf16[2,64,512]{2,1,0:T(8,128)(2,1)S(1)}, bf16[2,64,512]{2,1,0:T(8,128)(2,1)S(1)}, u32[]{:S(2)}, u32[]{:S(2)}) collective-permute-start(bf16[2,64,512]{2,1,0:T(8,128)(2,1)S(1)} %collective-permute-done.9.refs_10_), channel_id=1, source_target_pairs={{0,56},{8,0},{16,8},{24,16},{32,24},{40,32},{48,40},{56,48},{1,57}... | collective-permute-start | bytes 393224 | tf_op jit(solution)/shard_map/ppermute | solution.py:19
  16.0 3.5 %collective-permute-done.6.refs_6_ = bf16[2,64,512]{2,1,0:T(8,128)(2,1)S(1)} collective-permute-done((bf16[2,64,512]{2,1,0:T(8,128)(2,1)}, bf16[2,64,512]{2,1,0:T(8,128)(2,1)S(1)}, u32[]{:S(2)}, u32[]{:S(2)}) %collective-permute-start.6) | collective-permute-done | bytes 131104 | tf_op jit(solution)/shard_map/ppermute | solution.py:19
  19.5 0.0 collective-permute-start.8
  19.5 0.0 collective-permute-done.11.refs_11_
  19.5 0.0 collective-permute-start.7
  19.6 0.0 collective-permute-done.1.refs_0_
  19.6 8.2 %collective-permute-start.4 = (bf16[2,128,256]{2,1,0:T(8,128)(2,1)S(1)}, bf16[2,128,256]{2,1,0:T(8,128)(2,1)S(1)}, u32[]{:S(2)}, u32[]{:S(2)}) collective-permute-start(bf16[2,128,256]{2,1,0:T(8,128)(2,1)S(1)} %collective-permute-done.1.refs_0_), channel_id=1, source_target_pairs={{0,6},{2,0},{4,2},{6,4},{1,7},{3,1},{5,3},{7,5},{8,14},{10,8},{12,... | collective-permute-start | bytes 393224 | tf_op jit(solution)/shard_map/ppermute | solution.py:19
  27.8 0.0 collective-permute-done.5.refs_5_
  27.8 0.0 collective-permute-start.3
  27.8 0.0 collective-permute-done.10.refs_9_
  27.8 0.6 collective-permute-start.2
  28.4 0.0 collective-permute-done.8.refs_8_
  28.4 0.0 collective-permute-done.7.refs_7_
  28.4 5.1 %collective-permute-done.4.refs_3_ = bf16[2,128,256]{2,1,0:T(8,128)(2,1)S(1)} collective-permute-done((bf16[2,128,256]{2,1,0:T(8,128)(2,1)S(1)}, bf16[2,128,256]{2,1,0:T(8,128)(2,1)S(1)}, u32[]{:S(2)}, u32[]{:S(2)}) %collective-permute-start.4) | collective-permute-done | bytes 131104 | tf_op jit(solution)/shard_map/ppermute | solution.py:19
  33.5 0.0 collective-permute-done.3.refs_2_
  33.5 3.3 %collective-permute-done.2.refs_1_ = bf16[2,128,256]{2,1,0:T(8,128)(2,1)S(1)} collective-permute-done((bf16[2,128,256]{2,1,0:T(8,128)(2,1)S(1)}, bf16[2,128,256]{2,1,0:T(8,128)(2,1)S(1)}, u32[]{:S(2)}, u32[]{:S(2)}) %collective-permute-start.2) | collective-permute-done | bytes 131104 | tf_op jit(solution)/shard_map/ppermute | solution.py:19
  36.8 1.6 %predict.1 = (f32[128,512]{1,0:T(8,128)S(1)}, s16[144,512]{1,0:T(8,128)(2,1)S(1)}, s16[144,512]{1,0:T(8,128)(2,1)S(1)}, s16[144,512]{1,0:T(8,128)(2,1)S(1)}, bf1...) custom-call(s32[5]{0:T(128)S(1)} %stack.23.place.refs_0_, ...), custom_call_target="tpu_custom_call" | custom-call | tf_op jit(solution)/shard_map/predict/pallas_call | solution.py:210
  38.4 0.0 copy-start.3
  38.4 0.1 collective-permute-start.12
  38.5 0.1 collective-permute-start.13
  38.6 2.6 %collective-permute-start.14 = (s16[144,512]{1,0:T(8,128)(2,1)S(1)}, s16[144,512]{1,0:T(8,128)(2,1)S(1)}, u32[]{:S(2)}, u32[]{:S(2)}) collective-permute-start(s16[144,512]{1,0:T(8,128)(2,1)S(1)} %get-tuple-element.32), channel_id=1, source_target_pairs={{0,192},{64,0},{128,64},{192,128},{1,193},{65,1},{129,65},{193,129... | collective-permute-start | bytes 442376 | tf_op jit(solution)/shard_map/ppermute | solution.py:19
  41.1 6.6 %collective-permute-done.12.p1 = s16[144,512]{1,0:T(8,128)(2,1)S(1)} collective-permute-done((s16[144,512]{1,0:T(8,128)(2,1)S(1)}, s16[144,512]{1,0:T(8,128)(2,1)S(1)}, u32[]{:S(2)}, u32[]{:S(2)}) %collective-permute-start.12) | collective-permute-done | bytes 147488 | tf_op jit(solution)/shard_map/ppermute | solution.py:19
  47.7 0.0 collective-permute-done.13.p2
  47.7 0.0 collective-permute-done.14.p3
  47.7 1.4 %residual.1 = (f32[2,64,512]{2,1,0:T(8,128)}, s16[144,512]{1,0:T(8,128)(2,1)S(1)}) custom-call(s32[5]{0:T(128)S(1)} %stack.23.place.refs_0_, f32[128,512]{1,0:T(8,128)S(1)} %get-tuple-element.29.p0, s16[144,512]{1,0:T(8,128)(2,1)S(1)} %collective-permute-done.12.p1, s16[144,512]{1,0:T(8,128)(2,1)S(1)} %collective-permute-done.13.p2, ...), custom_call_target="tpu_custom_call" | custom-call | tf_op jit(solution)/shard_map/residual/pallas_call | solution.py:218
  49.2 3.2 %collective-permute-start.17 = (s16[144,512]{1,0:T(8,128)(2,1)S(1)}, s16[144,512]{1,0:T(8,128)(2,1)S(1)}, u32[]{:S(2)}, u32[]{:S(2)}) collective-permute-start(s16[144,512]{1,0:T(8,128)(2,1)S(1)} %get-tuple-element.36.e0), channel_id=1, source_target_pairs={{0,192},{64,0},{128,64},{192,128},{1,193},{65,1},{129,65},{193,129... | collective-permute-start | bytes 442376 | tf_op jit(solution)/shard_map/ppermute | solution.py:19
  52.3 0.0 collective-permute-start.16
  52.3 0.6 collective-permute-start.15
  52.9 5.3 %collective-permute-done.17.e3 = s16[144,512]{1,0:T(8,128)(2,1)S(1)} collective-permute-done((s16[144,512]{1,0:T(8,128)(2,1)S(1)}, s16[144,512]{1,0:T(8,128)(2,1)S(1)}, u32[]{:S(2)}, u32[]{:S(2)}) %collective-permute-start.17) | collective-permute-done | bytes 147488 | tf_op jit(solution)/shard_map/ppermute | solution.py:19
  58.3 0.0 collective-permute-done.16.e2
  58.3 3.9 %collective-permute-done.15.e1 = s16[144,512]{1,0:T(8,128)(2,1)S(1)} collective-permute-done((s16[144,512]{1,0:T(8,128)(2,1)S(1)}, s16[144,512]{1,0:T(8,128)(2,1)S(1)}, u32[]{:S(2)}, u32[]{:S(2)}) %collective-permute-start.15) | collective-permute-done | bytes 147488 | tf_op jit(solution)/shard_map/ppermute | solution.py:19
  62.1 3.4 %grads.1 = (f32[128,512]{1,0:T(8,128)S(1)}, f32[128,512]{1,0:T(8,128)S(1)}, f32[128,512]{1,0:T(8,128)S(1)}, s16[272,512]{1,0:T(8,128)(2,1)S(1)}, s16[272,512]{1,...) custom-call(s32[5]{0:T(128)S(1)} %stack.23.place.refs_0_, ...), custom_call_target="tpu_custom_call" | custom-call | tf_op jit(solution)/shard_map/grads/pallas_call | solution.py:222
  65.5 0.9 collective-permute-start.18
  66.4 0.2 collective-permute-start.22
  66.6 2.5 %collective-permute-start.23 = (s16[272,512]{1,0:T(8,128)(2,1)S(1)}, s16[272,512]{1,0:T(8,128)(2,1)S(1)}, u32[]{:S(2)}, u32[]{:S(2)}) collective-permute-start(s16[272,512]{1,0:T(8,128)(2,1)S(1)} %get-tuple-element.45), channel_id=1, source_target_pairs={{0,56},{8,0},{16,8},{24,16},{32,24},{40,32},{48,40},{56,48},{1,57}... | collective-permute-start | bytes 835592 | tf_op jit(solution)/shard_map/ppermute | solution.py:19
  69.1 0.0 collective-permute-done.18.other
  69.1 0.6 core_sum.1
  69.7 0.1 collective-permute-start.19
  69.8 1.0 %collective-permute-start.20 = (f32[128,256]{1,0:T(8,128)S(1)}, f32[128,256]{1,0:T(8,128)S(1)}, u32[]{:S(2)}, u32[]{:S(2)}) collective-permute-start(f32[128,256]{1,0:T(8,128)S(1)} %get-tuple-element.41), channel_id=1, source_target_pairs={{0,4},{2,6},{4,0},{6,2},{1,5},{3,7},{5,1},{7,3},{8,12},{10,14},{12... | collective-permute-start | bytes 393224 | tf_op jit(solution)/shard_map/ppermute | solution.py:19
  70.9 1.6 %collective-permute-start.21 = (f32[128,256]{1,0:T(8,128)S(1)}, f32[128,256]{1,0:T(8,128)S(1)}, u32[]{:S(2)}, u32[]{:S(2)}) collective-permute-start(f32[128,256]{1,0:T(8,128)S(1)} %get-tuple-element.42), channel_id=1, source_target_pairs={{0,6},{2,0},{4,2},{6,4},{1,7},{3,1},{5,3},{7,5},{8,14},{10,8},{12,... | collective-permute-start | bytes 393224 | tf_op jit(solution)/shard_map/ppermute | solution.py:19
  72.5 3.4 %collective-permute-done.22.up = s16[272,512]{1,0:T(8,128)(2,1)S(1)} collective-permute-done((s16[272,512]{1,0:T(8,128)(2,1)S(1)}, s16[272,512]{1,0:T(8,128)(2,1)S(1)}, u32[]{:S(2)}, u32[]{:S(2)}) %collective-permute-start.22) | collective-permute-done | bytes 278560 | tf_op jit(solution)/shard_map/ppermute | solution.py:19
  75.9 1.7 %collective-permute-start.26 = (s16[144,512]{1,0:T(8,128)(2,1)S(1)}, s16[144,512]{1,0:T(8,128)(2,1)S(1)}, u32[]{:S(2)}, u32[]{:S(2)}) collective-permute-start(s16[144,512]{1,0:T(8,128)(2,1)S(1)} %get-tuple-element.51), channel_id=1, source_target_pairs={{0,32},{8,40},{16,48},{24,56},{32,0},{40,8},{48,16},{56,24},{1,33}... | collective-permute-start | bytes 442376 | tf_op jit(solution)/shard_map/ppermute | solution.py:19
  77.6 0.7 relay.1
  78.4 1.9 %collective-permute-start.24 = (s16[144,512]{1,0:T(8,128)(2,1)S(1)}, s16[144,512]{1,0:T(8,128)(2,1)S(1)}, u32[]{:S(2)}, u32[]{:S(2)}) collective-permute-start(s16[144,512]{1,0:T(8,128)(2,1)S(1)} %get-tuple-element.49), channel_id=1, source_target_pairs={{0,16},{8,24},{16,32},{24,40},{32,48},{40,56},{48,0},{56,8},{1,17}... | collective-permute-start | bytes 442376 | tf_op jit(solution)/shard_map/ppermute | solution.py:19
  80.3 0.0 collective-permute-done.19.s1
  80.3 1.7 %collective-permute-start.25 = (s16[144,512]{1,0:T(8,128)(2,1)S(1)}, s16[144,512]{1,0:T(8,128)(2,1)S(1)}, u32[]{:S(2)}, u32[]{:S(2)}) collective-permute-start(s16[144,512]{1,0:T(8,128)(2,1)S(1)} %get-tuple-element.50), channel_id=1, source_target_pairs={{0,48},{8,56},{16,0},{24,8},{32,16},{40,24},{48,32},{56,40},{1,49}... | collective-permute-start | bytes 442376 | tf_op jit(solution)/shard_map/ppermute | solution.py:19
  82.0 0.6 refl_sum.1
  82.7 0.7 collective-permute-start.27
  83.3 3.6 %collective-permute-done.26.refs_4_ = s16[144,512]{1,0:T(8,128)(2,1)S(1)} collective-permute-done((s16[144,512]{1,0:T(8,128)(2,1)S(1)}, s16[144,512]{1,0:T(8,128)(2,1)S(1)}, u32[]{:S(2)}, u32[]{:S(2)}) %collective-permute-start.26) | collective-permute-done | bytes 147488 | tf_op jit(solution)/shard_map/ppermute | solution.py:19
  86.9 1.5 %collective-permute-done.24.refs_2_ = s16[144,512]{1,0:T(8,128)(2,1)S(1)} collective-permute-done((s16[144,512]{1,0:T(8,128)(2,1)S(1)}, s16[144,512]{1,0:T(8,128)(2,1)S(1)}, u32[]{:S(2)}, u32[]{:S(2)}) %collective-permute-start.24) | collective-permute-done | bytes 147488 | tf_op jit(solution)/shard_map/ppermute | solution.py:19
  88.4 5.3 %collective-permute-done.25.refs_3_ = s16[144,512]{1,0:T(8,128)(2,1)S(1)} collective-permute-done((s16[144,512]{1,0:T(8,128)(2,1)S(1)}, s16[144,512]{1,0:T(8,128)(2,1)S(1)}, u32[]{:S(2)}, u32[]{:S(2)}) %collective-permute-start.25) | collective-permute-done | bytes 147488 | tf_op jit(solution)/shard_map/ppermute | solution.py:19
  93.7 1.4 %last.1 = (f32[2,64,512]{2,1,0:T(8,128)}, f32[2,64,256]{2,1,0:T(8,128)}) custom-call(s32[5]{0:T(128)S(1)} %stack.23.place.refs_0_, f32[128,512]{1,0:T(8,128)S(1)} %get-tuple-element.46.refs_1_, s16[144,512]{1,0:T(8,128)(2,1)S(1)} %collective-permute-done.24.refs_2_, s16[144,512]{1,0:T(8,128)(2,1)S(1)} %collective-permute-done.25.refs_3_, ...), custom_call_target="tpu_custom_call" | custom-call | tf_op jit(solution)/shard_map/last/pallas_call | solution.py:251
  (9 shorter events, 0.0 us)
Async XLA Ops:
  0.6 12.3 %collective-permute-start.9 = (bf16[2,64,512]{2,1,0:T(8,128)(2,1)}, bf16[2,64,512]{2,1,0:T(8,128)(2,1)S(1)}, u32[]{:S(2)}, u32[]{:S(2)}) collective-permute-start(bf16[2,64,512]{2,1,0:T(8,128)(2,1)} %bitcast.17), channel_id=1, source_target_pairs={{0,48},{8,56},{16,0},{24,8},{32,16},{40,24},{48,32},{56,40},{1,49}... | collective-permute-start | bytes 393224 | tf_op jit(solution)/shard_map/ppermute | solution.py:19
  7.6 3.0 %collective-permute-start = (bf16[2,64,256]{2,1,0:T(8,128)(2,1)}, bf16[2,64,256]{2,1,0:T(8,128)(2,1)S(1)}, u32[]{:S(2)}, u32[]{:S(2)}) collective-permute-start(bf16[2,64,256]{2,1,0:T(8,128)(2,1)} %bitcast.23), channel_id=1, source_target_pairs={{0,1},{1,0},{2,3},{3,2},{4,5},{5,4},{6,7},{7,6},{8,9},{9,8},{10,11... | collective-permute-start | bytes 196616 | tf_op jit(solution)/shard_map/ppermute | solution.py:19
  8.5 11.0 %collective-permute-start.11 = (bf16[2,64,512]{2,1,0:T(8,128)(2,1)}, bf16[2,64,512]{2,1,0:T(8,128)(2,1)S(1)}, u32[]{:S(2)}, u32[]{:S(2)}) collective-permute-start(bf16[2,64,512]{2,1,0:T(8,128)(2,1)} %bitcast.18), channel_id=1, source_target_pairs={{0,56},{8,0},{16,8},{24,16},{32,24},{40,32},{48,40},{56,48},{1,57}... | collective-permute-start | bytes 393224 | tf_op jit(solution)/shard_map/ppermute | solution.py:19
  9.2 10.3 %collective-permute-start.6 = (bf16[2,64,512]{2,1,0:T(8,128)(2,1)}, bf16[2,64,512]{2,1,0:T(8,128)(2,1)S(1)}, u32[]{:S(2)}, u32[]{:S(2)}) collective-permute-start(bf16[2,64,512]{2,1,0:T(8,128)(2,1)} %bitcast.19), channel_id=1, source_target_pairs={{0,16},{8,24},{16,32},{24,40},{32,48},{40,56},{48,0},{56,8},{1,17}... | collective-permute-start | bytes 393224 | tf_op jit(solution)/shard_map/ppermute | solution.py:19
  10.5 2.3 %copy-start = (bf16[2,1,64,512]{3,2,1,0:T(8,128)(2,1)S(1)}, bf16[2,1,64,512]{3,2,1,0:T(8,128)(2,1)}, u32[]{:S(2)}) copy-start(bf16[2,1,64,512]{3,2,1,0:T(8,128)(2,1)} %param.5) | copy-start | bytes 393220
  10.5 0.9 copy-start.2
  12.0 35.8 %copy-start.1 = (bf16[2,1,64,512]{3,2,1,0:T(8,128)(2,1)S(1)}, bf16[2,1,64,512]{3,2,1,0:T(8,128)(2,1)}, u32[]{:S(2)}) copy-start(bf16[2,1,64,512]{3,2,1,0:T(8,128)(2,1)} %param.6) | copy-start | bytes 393220
  12.0 7.6 %collective-permute-start.1 = (bf16[2,128,256]{2,1,0:T(8,128)(2,1)S(1)}, bf16[2,128,256]{2,1,0:T(8,128)(2,1)S(1)}, u32[]{:S(2)}, u32[]{:S(2)}) collective-permute-start(bf16[2,128,256]{2,1,0:T(8,128)(2,1)S(1)} %pair.1), channel_id=1, source_target_pairs={{0,0},{2,64},{4,128},{6,192},{64,2},{66,66},{68,130},{70,194},{128... | collective-permute-start | bytes 393224 | tf_op jit(solution)/shard_map/ppermute | solution.py:24
  12.8 15.0 %collective-permute-start.5 = (bf16[2,64,512]{2,1,0:T(8,128)(2,1)S(1)}, bf16[2,64,512]{2,1,0:T(8,128)(2,1)S(1)}, u32[]{:S(2)}, u32[]{:S(2)}) collective-permute-start(bf16[2,64,512]{2,1,0:T(8,128)(2,1)S(1)} %bitcast.20), channel_id=1, source_target_pairs={{0,8},{8,16},{16,24},{24,32},{32,40},{40,48},{48,56},{56,0},{1,9},... | collective-permute-start | bytes 393224 | tf_op jit(solution)/shard_map/ppermute | solution.py:19
  12.9 14.9 %collective-permute-start.10 = (bf16[2,64,512]{2,1,0:T(8,128)(2,1)S(1)}, bf16[2,64,512]{2,1,0:T(8,128)(2,1)S(1)}, u32[]{:S(2)}, u32[]{:S(2)}) collective-permute-start(bf16[2,64,512]{2,1,0:T(8,128)(2,1)S(1)} %collective-permute-done.9.refs_10_), channel_id=1, source_target_pairs={{0,56},{8,0},{16,8},{24,16},{32,24},{40,32},{48,40},{56,48},{1,57}... | collective-permute-start | bytes 393224 | tf_op jit(solution)/shard_map/ppermute | solution.py:19
  19.5 8.9 %collective-permute-start.8 = (bf16[2,64,512]{2,1,0:T(8,128)(2,1)S(1)}, bf16[2,64,512]{2,1,0:T(8,128)(2,1)S(1)}, u32[]{:S(2)}, u32[]{:S(2)}) collective-permute-start(bf16[2,64,512]{2,1,0:T(8,128)(2,1)S(1)} %collective-permute-done.6.refs_6_), channel_id=1, source_target_pairs={{0,16},{8,24},{16,32},{24,40},{32,48},{40,56},{48,0},{56,8},{1,17}... | collective-permute-start | bytes 393224 | tf_op jit(solution)/shard_map/ppermute | solution.py:19
  19.5 8.8 %collective-permute-start.7 = (bf16[2,64,512]{2,1,0:T(8,128)(2,1)S(1)}, bf16[2,64,512]{2,1,0:T(8,128)(2,1)S(1)}, u32[]{:S(2)}, u32[]{:S(2)}) collective-permute-start(bf16[2,64,512]{2,1,0:T(8,128)(2,1)S(1)} %collective-permute-done.6.refs_6_), channel_id=1, source_target_pairs={{0,8},{8,16},{16,24},{24,32},{32,40},{40,48},{48,56},{56,0},{1,9},... | collective-permute-start | bytes 393224 | tf_op jit(solution)/shard_map/ppermute | solution.py:19
  19.6 13.9 %collective-permute-start.4 = (bf16[2,128,256]{2,1,0:T(8,128)(2,1)S(1)}, bf16[2,128,256]{2,1,0:T(8,128)(2,1)S(1)}, u32[]{:S(2)}, u32[]{:S(2)}) collective-permute-start(bf16[2,128,256]{2,1,0:T(8,128)(2,1)S(1)} %collective-permute-done.1.refs_0_), channel_id=1, source_target_pairs={{0,6},{2,0},{4,2},{6,4},{1,7},{3,1},{5,3},{7,5},{8,14},{10,8},{12,... | collective-permute-start | bytes 393224 | tf_op jit(solution)/shard_map/ppermute | solution.py:19
  27.8 5.7 %collective-permute-start.3 = (bf16[2,128,256]{2,1,0:T(8,128)(2,1)S(1)}, bf16[2,128,256]{2,1,0:T(8,128)(2,1)S(1)}, u32[]{:S(2)}, u32[]{:S(2)}) collective-permute-start(bf16[2,128,256]{2,1,0:T(8,128)(2,1)S(1)} %collective-permute-done.1.refs_0_), channel_id=1, source_target_pairs={{0,4},{2,6},{4,0},{6,2},{1,5},{3,7},{5,1},{7,3},{8,12},{10,14},{12... | collective-permute-start | bytes 393224 | tf_op jit(solution)/shard_map/ppermute | solution.py:19
  27.8 9.0 %collective-permute-start.2 = (bf16[2,128,256]{2,1,0:T(8,128)(2,1)S(1)}, bf16[2,128,256]{2,1,0:T(8,128)(2,1)S(1)}, u32[]{:S(2)}, u32[]{:S(2)}) collective-permute-start(bf16[2,128,256]{2,1,0:T(8,128)(2,1)S(1)} %collective-permute-done.1.refs_0_), channel_id=1, source_target_pairs={{0,2},{2,4},{4,6},{6,0},{1,3},{3,5},{5,7},{7,1},{8,10},{10,12},{12... | collective-permute-start | bytes 393224 | tf_op jit(solution)/shard_map/ppermute | solution.py:19
  38.4 9.4 %copy-start.3 = (s32[8,20]{1,0:T(8,128)S(1)}, s32[8,20]{1,0:T(8,128)}, u32[]{:S(2)}) copy-start(s32[8,20]{1,0:T(8,128)} %rec.1) | copy-start | bytes 1924
  38.4 9.3 %collective-permute-start.12 = (s16[144,512]{1,0:T(8,128)(2,1)S(1)}, s16[144,512]{1,0:T(8,128)(2,1)S(1)}, u32[]{:S(2)}, u32[]{:S(2)}) collective-permute-start(s16[144,512]{1,0:T(8,128)(2,1)S(1)} %get-tuple-element.30), channel_id=1, source_target_pairs={{0,64},{64,128},{128,192},{192,0},{1,65},{65,129},{129,193},{193,1... | collective-permute-start | bytes 442376 | tf_op jit(solution)/shard_map/ppermute | solution.py:19
  38.5 9.2 %collective-permute-start.13 = (s16[144,512]{1,0:T(8,128)(2,1)S(1)}, s16[144,512]{1,0:T(8,128)(2,1)S(1)}, u32[]{:S(2)}, u32[]{:S(2)}) collective-permute-start(s16[144,512]{1,0:T(8,128)(2,1)S(1)} %get-tuple-element.31), channel_id=1, source_target_pairs={{0,128},{64,192},{128,0},{192,64},{1,129},{65,193},{129,1},{193,65... | collective-permute-start | bytes 442376 | tf_op jit(solution)/shard_map/ppermute | solution.py:19
  38.6 9.1 %collective-permute-start.14 = (s16[144,512]{1,0:T(8,128)(2,1)S(1)}, s16[144,512]{1,0:T(8,128)(2,1)S(1)}, u32[]{:S(2)}, u32[]{:S(2)}) collective-permute-start(s16[144,512]{1,0:T(8,128)(2,1)S(1)} %get-tuple-element.32), channel_id=1, source_target_pairs={{0,192},{64,0},{128,64},{192,128},{1,193},{65,1},{129,65},{193,129... | collective-permute-start | bytes 442376 | tf_op jit(solution)/shard_map/ppermute | solution.py:19
  49.2 9.1 %collective-permute-start.17 = (s16[144,512]{1,0:T(8,128)(2,1)S(1)}, s16[144,512]{1,0:T(8,128)(2,1)S(1)}, u32[]{:S(2)}, u32[]{:S(2)}) collective-permute-start(s16[144,512]{1,0:T(8,128)(2,1)S(1)} %get-tuple-element.36.e0), channel_id=1, source_target_pairs={{0,192},{64,0},{128,64},{192,128},{1,193},{65,1},{129,65},{193,129... | collective-permute-start | bytes 442376 | tf_op jit(solution)/shard_map/ppermute | solution.py:19
  52.3 5.9 %collective-permute-start.16 = (s16[144,512]{1,0:T(8,128)(2,1)S(1)}, s16[144,512]{1,0:T(8,128)(2,1)S(1)}, u32[]{:S(2)}, u32[]{:S(2)}) collective-permute-start(s16[144,512]{1,0:T(8,128)(2,1)S(1)} %get-tuple-element.36.e0), channel_id=1, source_target_pairs={{0,128},{64,192},{128,0},{192,64},{1,129},{65,193},{129,1},{193,65... | collective-permute-start | bytes 442376 | tf_op jit(solution)/shard_map/ppermute | solution.py:19
  52.3 9.8 %collective-permute-start.15 = (s16[144,512]{1,0:T(8,128)(2,1)S(1)}, s16[144,512]{1,0:T(8,128)(2,1)S(1)}, u32[]{:S(2)}, u32[]{:S(2)}) collective-permute-start(s16[144,512]{1,0:T(8,128)(2,1)S(1)} %get-tuple-element.36.e0), channel_id=1, source_target_pairs={{0,64},{64,128},{128,192},{192,0},{1,65},{65,129},{129,193},{193,1... | collective-permute-start | bytes 442376 | tf_op jit(solution)/shard_map/ppermute | solution.py:19
  65.5 3.6 %collective-permute-start.18 = (f32[4,128,256]{2,1,0:T(8,128)S(1)}, f32[4,128,256]{2,1,0:T(8,128)S(1)}, u32[]{:S(2)}, u32[]{:S(2)}) collective-permute-start(f32[4,128,256]{2,1,0:T(8,128)S(1)} %get-tuple-element.38), channel_id=1, source_target_pairs={{0,1},{1,0},{2,3},{3,2},{4,5},{5,4},{6,7},{7,6},{8,9},{9,8},{10,11... | collective-permute-start | bytes 1572872 | tf_op jit(solution)/shard_map/ppermute | solution.py:19
  66.4 9.4 %collective-permute-start.22 = (s16[272,512]{1,0:T(8,128)(2,1)S(1)}, s16[272,512]{1,0:T(8,128)(2,1)S(1)}, u32[]{:S(2)}, u32[]{:S(2)}) collective-permute-start(s16[272,512]{1,0:T(8,128)(2,1)S(1)} %get-tuple-element.44), channel_id=1, source_target_pairs={{0,8},{8,16},{16,24},{24,32},{32,40},{40,48},{48,56},{56,0},{1,9},... | collective-permute-start | bytes 835592 | tf_op jit(solution)/shard_map/ppermute | solution.py:19
  66.6 11.0 %collective-permute-start.23 = (s16[272,512]{1,0:T(8,128)(2,1)S(1)}, s16[272,512]{1,0:T(8,128)(2,1)S(1)}, u32[]{:S(2)}, u32[]{:S(2)}) collective-permute-start(s16[272,512]{1,0:T(8,128)(2,1)S(1)} %get-tuple-element.45), channel_id=1, source_target_pairs={{0,56},{8,0},{16,8},{24,16},{32,24},{40,32},{48,40},{56,48},{1,57}... | collective-permute-start | bytes 835592 | tf_op jit(solution)/shard_map/ppermute | solution.py:19
  69.7 10.5 %collective-permute-start.19 = (f32[128,256]{1,0:T(8,128)S(1)}, f32[128,256]{1,0:T(8,128)S(1)}, u32[]{:S(2)}, u32[]{:S(2)}) collective-permute-start(f32[128,256]{1,0:T(8,128)S(1)} %get-tuple-element.40), channel_id=1, source_target_pairs={{0,2},{2,4},{4,6},{6,0},{1,3},{3,5},{5,7},{7,1},{8,10},{10,12},{12... | collective-permute-start | bytes 393224 | tf_op jit(solution)/shard_map/ppermute | solution.py:19
  69.8 12.2 %collective-permute-start.20 = (f32[128,256]{1,0:T(8,128)S(1)}, f32[128,256]{1,0:T(8,128)S(1)}, u32[]{:S(2)}, u32[]{:S(2)}) collective-permute-start(f32[128,256]{1,0:T(8,128)S(1)} %get-tuple-element.41), channel_id=1, source_target_pairs={{0,4},{2,6},{4,0},{6,2},{1,5},{3,7},{5,1},{7,3},{8,12},{10,14},{12... | collective-permute-start | bytes 393224 | tf_op jit(solution)/shard_map/ppermute | solution.py:19
  70.9 11.1 %collective-permute-start.21 = (f32[128,256]{1,0:T(8,128)S(1)}, f32[128,256]{1,0:T(8,128)S(1)}, u32[]{:S(2)}, u32[]{:S(2)}) collective-permute-start(f32[128,256]{1,0:T(8,128)S(1)} %get-tuple-element.42), channel_id=1, source_target_pairs={{0,6},{2,0},{4,2},{6,4},{1,7},{3,1},{5,3},{7,5},{8,14},{10,8},{12,... | collective-permute-start | bytes 393224 | tf_op jit(solution)/shard_map/ppermute | solution.py:19
  75.9 11.1 %collective-permute-start.26 = (s16[144,512]{1,0:T(8,128)(2,1)S(1)}, s16[144,512]{1,0:T(8,128)(2,1)S(1)}, u32[]{:S(2)}, u32[]{:S(2)}) collective-permute-start(s16[144,512]{1,0:T(8,128)(2,1)S(1)} %get-tuple-element.51), channel_id=1, source_target_pairs={{0,32},{8,40},{16,48},{24,56},{32,0},{40,8},{48,16},{56,24},{1,33}... | collective-permute-start | bytes 442376 | tf_op jit(solution)/shard_map/ppermute | solution.py:19
  78.4 10.1 %collective-permute-start.24 = (s16[144,512]{1,0:T(8,128)(2,1)S(1)}, s16[144,512]{1,0:T(8,128)(2,1)S(1)}, u32[]{:S(2)}, u32[]{:S(2)}) collective-permute-start(s16[144,512]{1,0:T(8,128)(2,1)S(1)} %get-tuple-element.49), channel_id=1, source_target_pairs={{0,16},{8,24},{16,32},{24,40},{32,48},{40,56},{48,0},{56,8},{1,17}... | collective-permute-start | bytes 442376 | tf_op jit(solution)/shard_map/ppermute | solution.py:19
  80.3 13.4 %collective-permute-start.25 = (s16[144,512]{1,0:T(8,128)(2,1)S(1)}, s16[144,512]{1,0:T(8,128)(2,1)S(1)}, u32[]{:S(2)}, u32[]{:S(2)}) collective-permute-start(s16[144,512]{1,0:T(8,128)(2,1)S(1)} %get-tuple-element.50), channel_id=1, source_target_pairs={{0,48},{8,56},{16,0},{24,8},{32,16},{40,24},{48,32},{56,40},{1,49}... | collective-permute-start | bytes 442376 | tf_op jit(solution)/shard_map/ppermute | solution.py:19
  82.7 11.0 %collective-permute-start.27 = (f32[128,256]{1,0:T(8,128)S(1)}, f32[128,256]{1,0:T(8,128)S(1)}, u32[]{:S(2)}, u32[]{:S(2)}) collective-permute-start(f32[128,256]{1,0:T(8,128)S(1)} %get-tuple-element.52), channel_id=1, source_target_pairs={{0,0},{2,64},{4,128},{6,192},{64,2},{66,66},{68,130},{70,194},{128... | collective-permute-start | bytes 393224 | tf_op jit(solution)/shard_map/ppermute | solution.py:24
